TPU v7x, 32 devices: a whole 2x2x4 slice. The times are simulated.
32 devices in a mesh: row: 4 (over y, core), col: 8 (over z, x).
Axes of the slice: x: 2, y: 2, z: 4, core: 2. Of those that a mesh axis runs over, the one named last changes fastest.
Arguments:
- tokens: bfloat16 [128, 12288], P('col', 'row'), may hold values from -6 to 6
- norm_gain: float32 [12288], P('row'), may hold values from 0.25 to 90
- norm_bias: float32 [12288], P('row'), may hold values from -3 to 3
- weight_in: bfloat16 [12288, 24576], P('row', 'col'), may hold values from -1 to 1
- weight_out: bfloat16 [24576, 12288], P('col', 'row'), may hold values from -0.0390625 to 0.0390625
- cotangent: bfloat16 [128, 12288], P('col', 'row'), may hold values from -6 to 6
Outputs:
- output: bfloat16 [128, 12288], P('col', 'row')
- input_grad: bfloat16 [128, 12288], P('col', 'row')
- first_grad: bfloat16 [12288, 24576], P('row', 'col')
- second_grad: bfloat16 [24576, 12288], P('col', 'row')
- gain_grad: float32 [12288], P('row')
- bias_grad: float32 [12288], P('row')
All inputs are finite; a program needn't handle non-finite values.
Results may differ from a plain program's by a relative error of at most 0.018.
Values may be sent and summed in bfloat16 or wider, within the bound.
A program may use at most 320 MiB of HBM per device.

v0:
```python
import jax
import jax.numpy as jnp
from jax import lax
from jax.sharding import PartitionSpec as P

D = 12288
FF = 24576


gelu_scale = 0.7978845608028654
cubic = 0.044715
epsilon = 1e-05


def gelu(value):
    return 0.5 * value * (1.0 + jnp.tanh(gelu_scale * (value + cubic * value * value * value)))


def gelu_slope(value):
    inner = jnp.tanh(gelu_scale * (value + cubic * value * value * value))
    return 0.5 * (1.0 + inner) + 0.5 * value * (1.0 - inner * inner) * gelu_scale * (
        1.0 + 3.0 * cubic * value * value
    )


def transposed_product(left, right):
    return lax.dot_general(
        left, right, (((1,), (1,)), ((), ())), preferred_element_type=jnp.float32
    )


def per_device(tokens, norm_gain, norm_bias, weight_in, weight_out, cotangent):
    features = tokens.shape[1] * lax.axis_size("row")
    widened = tokens.astype(jnp.float32)
    row_total = lax.psum(jnp.sum(widened, axis=1), "row")
    center = widened - (row_total / features)[:, None]
    variance = lax.psum(jnp.sum(center * center, axis=1), "row") / features
    inverse = lax.rsqrt(variance + epsilon)
    normal = center * inverse[:, None]
    normed = (normal * norm_gain + norm_bias).astype(jnp.bfloat16)
    normed_all = lax.all_gather(normed, "col", axis=0, tiled=True)
    hidden = lax.psum_scatter(
        jnp.dot(normed_all, weight_in, preferred_element_type=jnp.float32).astype(jnp.bfloat16),
        "row",
        scatter_dimension=0,
        tiled=True,
    ).astype(jnp.float32)
    activation_all = lax.all_gather(gelu(hidden).astype(jnp.bfloat16), "row", axis=0, tiled=True)
    slope = gelu_slope(hidden)
    mixed = lax.psum_scatter(
        jnp.dot(activation_all, weight_out, preferred_element_type=jnp.float32).astype(
            jnp.bfloat16
        ),
        "col",
        scatter_dimension=0,
        tiled=True,
    ).astype(jnp.float32)
    output = (widened + mixed).astype(jnp.bfloat16)
    cotangent_all = lax.all_gather(cotangent, "col", axis=0, tiled=True)
    grad_act = lax.psum_scatter(
        transposed_product(cotangent_all, weight_out).astype(jnp.bfloat16),
        "row",
        scatter_dimension=0,
        tiled=True,
    ).astype(jnp.float32)
    grad_hidden_all = lax.all_gather(
        (grad_act * slope).astype(jnp.bfloat16), "row", axis=0, tiled=True
    )
    grad_normed = lax.psum_scatter(
        transposed_product(grad_hidden_all, weight_in).astype(jnp.bfloat16),
        "col",
        scatter_dimension=0,
        tiled=True,
    ).astype(jnp.float32)
    first = lax.dot_general(
        normed_all, grad_hidden_all, (((0,), (0,)), ((), ())), preferred_element_type=jnp.float32
    )
    second = lax.dot_general(
        activation_all, cotangent_all, (((0,), (0,)), ((), ())), preferred_element_type=jnp.float32
    )
    scaled = grad_normed * norm_gain
    sum_one, sum_two = lax.psum((jnp.sum(scaled, axis=1), jnp.sum(scaled * normal, axis=1)), "row")
    input_grad = (
        cotangent.astype(jnp.float32)
        + inverse[:, None]
        * (scaled - (sum_one / features)[:, None] - normal * (sum_two / features)[:, None])
    ).astype(jnp.bfloat16)
    gain_part, bias_part = lax.psum(
        (jnp.sum(grad_normed * normal, axis=0), jnp.sum(grad_normed, axis=0)), "col"
    )
    squares = lax.psum(jnp.sum(first * first) + jnp.sum(second * second), ("row", "col"))
    factor = jnp.minimum(1.0, jnp.sqrt(2.0 * D * FF / squares))
    return (
        output,
        input_grad,
        (first * factor).astype(jnp.bfloat16),
        (second * factor).astype(jnp.bfloat16),
        gain_part * factor,
        bias_part * factor,
    )


def solution(mesh):
    in_specs = (
        P("col", "row"),
        P("row"),
        P("row"),
        P("row", "col"),
        P("col", "row"),
        P("col", "row"),
    )
    out_specs = (
        P("col", "row"),
        P("col", "row"),
        P("row", "col"),
        P("col", "row"),
        P("row"),
        P("row"),
    )
    return jax.shard_map(
        per_device, mesh=mesh, in_specs=in_specs, out_specs=out_specs, check_vma=False
    )
```

profile of v0, /device:TPU:0, one launch (start us, length us, event | category | flops | bytes accessed | tf_op | source)
XLA Modules:
  0.0 339.4 jit_solution(15999602261188029454)
XLA Ops:
  7.2 0.0 copy-start
  7.2 0.0 copy-start.2
  7.2 0.0 copy-start.3
  7.2 0.0 reduce-scatter.9.cloned.1.call-start
  7.2 34.0 %all_gather.14 = bf16[128,3072]{1,0:T(8,128)(2,1)S(1)} all-gather(bf16[16,3072]{1,0:T(8,128)(2,1)} %param.11), channel_id=1, replica_groups=mesh['row'=4,'col'=8] {'col'}, dimensions={0}, use_global_device_ids=true | all-gather | bytes 884736 | tf_op jit(solution)/shard_map/all_gather | solution.py:59
  41.3 13.6 %convolution_convert_fusion.1 = bf16[128,3072]{1,0:T(8,128)(2,1)} fusion(bf16[128,3072]{1,0:T(8,128)(2,1)S(1)} %all_gather.14, bf16[3072,3072]{1,0:T(8,128)(2,1)} %param.10), kind=kOutput, calls=%fused_computation.5 | convolution fusion | flops 2416312320 | bytes 20447232 | tf_op jit(solution)/shard_map/dot_general | solution.py:27
  54.8 0.0 reduce-scatter.9.cloned.1.call-update
  54.9 0.0 reduce-scatter.5.cloned.1.call-start
  54.9 0.0 copy-done
  54.9 0.1 convert_reduce_fusion.1
  55.1 5.7 %psum.49 = f32[16]{0:T(128)S(1)} all-reduce(f32[16]{0:T(128)S(1)} %convert_reduce_fusion.1), channel_id=1, replica_groups=mesh['row'=4,'col'=8] {'row'}, use_global_device_ids=true, to_apply=%region_1.0 | all-reduce | flops 16 | bytes 128 | tf_op jit(solution)/shard_map/psum | solution.py:35
  60.7 0.2 fusion.24
  60.9 6.6 %psum.50 = f32[16]{0:T(128)S(1)} all-reduce(f32[16]{0:T(128)S(1)} %fusion.24), channel_id=1, replica_groups=mesh['row'=4,'col'=8] {'row'}, use_global_device_ids=true, to_apply=%region_3.0 | all-reduce | flops 16 | bytes 128 | tf_op jit(solution)/shard_map/psum | solution.py:37
  67.6 0.0 copy-done.2
  67.6 0.0 copy-done.3
  67.6 0.1 fusion.19
  67.7 32.2 %all_gather.12 = bf16[128,3072]{1,0:T(8,128)(2,1)S(1)} all-gather(bf16[16,3072]{1,0:T(8,128)(2,1)S(1)} %fusion.19), channel_id=1, replica_groups=mesh['row'=4,'col'=8] {'col'}, dimensions={0}, use_global_device_ids=true | all-gather | bytes 884736 | tf_op jit(solution)/shard_map/all_gather | solution.py:41
  100.0 9.9 %convolution_convert_fusion.3 = bf16[128,3072]{1,0:T(8,128)(2,1)} fusion(bf16[128,3072]{1,0:T(8,128)(2,1)S(1)} %all_gather.12, bf16[3072,3072]{1,0:T(8,128)(2,1)} %param.9), kind=kOutput, calls=%fused_computation.7 | convolution fusion | flops 2416312320 | bytes 20447232 | tf_op jit(solution)/shard_map/dot_general | solution.py:43
  109.8 0.0 reduce-scatter.5.cloned.1.call-update
  109.8 0.0 reduce-scatter.11.cloned.1.call-start
  109.9 0.0 reduce-scatter.9.cloned.1.call-done
  109.9 23.5 %reduce-scatter.5.cloned.1.call-done = bf16[32,3072]{1,0:T(8,128)(2,1)} async-done(((bf16[128,3072]{1,0:T(8,128)(2,1)}), bf16[32,3072]{1,0:T(8,128)(2,1)}) %reduce-scatter.5.cloned.1.call-update) | async-done | bytes 196624 | tf_op jit(solution)/shard_map/reduce_scatter | solution.py:42
  133.4 1.3 fusion.7
  134.7 8.4 %all_gather.15 = bf16[128,3072]{1,0:T(8,128)(2,1)S(1)} all-gather(bf16[32,3072]{1,0:T(8,128)(2,1)S(1)} %get-tuple-element.14), channel_id=1, replica_groups=mesh['row'=4,'col'=8] {'row'}, dimensions={0}, use_global_device_ids=true | all-gather | bytes 983040 | tf_op jit(solution)/shard_map/all_gather | solution.py:66
  143.1 13.6 %convolution_convert_fusion = bf16[128,3072]{1,0:T(8,128)(2,1)} fusion(bf16[128,3072]{1,0:T(8,128)(2,1)S(1)} %all_gather.15, bf16[3072,3072]{1,0:T(8,128)(2,1)} %param.9), kind=kOutput, calls=%fused_computation.4 | convolution fusion | flops 2416312320 | bytes 20447232 | tf_op jit(solution)/shard_map/dot_general | solution.py:27
  156.7 15.3 %multiply_reduce_fusion.1 = (f32[]{:T(128)}, f32[3072,3072]{1,0:T(8,128)}) fusion(bf16[128,3072]{1,0:T(8,128)(2,1)S(1)} %all_gather.12, bf16[128,3072]{1,0:T(8,128)(2,1)S(1)} %all_gather.15), kind=kOutput, calls=%fused_computation.3 | convolution fusion | flops 2434793472 | bytes 39321604 | tf_op jit(solution)/shard_map/dot_general | solution.py:75
  172.0 8.7 %all_gather.13 = bf16[128,3072]{1,0:T(8,128)(2,1)S(1)} all-gather(bf16[32,3072]{1,0:T(8,128)(2,1)S(1)} %get-tuple-element.15), channel_id=1, replica_groups=mesh['row'=4,'col'=8] {'row'}, dimensions={0}, use_global_device_ids=true | all-gather | bytes 983040 | tf_op jit(solution)/shard_map/all_gather | solution.py:48
  180.7 0.0 reduce-scatter.11.cloned.1.call-update
  180.7 0.3 reduce-scatter.7.cloned.1.call-start
  181.0 15.4 %multiply_reduce_fusion = (f32[]{:T(128)}, f32[3072,3072]{1,0:T(8,128)}) fusion(bf16[128,3072]{1,0:T(8,128)(2,1)S(1)} %all_gather.13, bf16[128,3072]{1,0:T(8,128)(2,1)S(1)} %all_gather.14), kind=kOutput, calls=%fused_computation.2 | convolution fusion | flops 2434793472 | bytes 39321604 | tf_op jit(solution)/shard_map/dot_general | solution.py:78
  197.7 39.8 %psum.53 = f32[]{:T(128)} all-reduce(f32[]{:T(128)S(6)} %add.65), channel_id=1, replica_groups=mesh['row'=4,'col'=8] {'row','col'}, use_global_device_ids=true, to_apply=%region_14.0 | all-reduce | flops 1 | bytes 8 | tf_op jit(solution)/shard_map/psum | solution.py:91
  238.2 9.9 %convolution_convert_fusion.2 = bf16[128,3072]{1,0:T(8,128)(2,1)} fusion(bf16[128,3072]{1,0:T(8,128)(2,1)S(1)} %all_gather.13, bf16[3072,3072]{1,0:T(8,128)(2,1)} %param.10), kind=kOutput, calls=%fused_computation.6 | convolution fusion | flops 2416312320 | bytes 20447232 | tf_op jit(solution)/shard_map/dot_general | solution.py:51
  248.1 0.0 reduce-scatter.7.cloned.1.call-update
  248.1 0.0 copy-start.1
  248.2 38.7 %multiply_convert_fusion = (bf16[3072,3072]{1,0:T(8,128)(2,1)}, bf16[3072,3072]{1,0:T(8,128)(2,1)}) fusion(f32[3072,3072]{1,0:T(8,128)} %get-tuple-element.21, f32[]{:T(128)S(6)} %min.3, f32[3072,3072]{1,0:T(8,128)} %get-tuple-element.19), kind=kLoop, calls=%fused_computation | loop fusion | flops 37748736 | bytes 113246208 | tf_op jit(solution)/shard_map/convert_element_type | solution.py:97
  286.8 0.0 reduce-scatter.11.cloned.1.call-done
  286.8 1.2 fusion.27
  288.0 6.4 %all-reduce.1 = (f32[16]{0:T(128)S(1)}, f32[16]{0:T(128)S(1)}) all-reduce(f32[16]{0:T(128)S(1)} %get-tuple-element.7, f32[16]{0:T(128)S(1)} %get-tuple-element.8), channel_id=1, replica_groups=mesh['row'=4,'col'=8] {'row'}, use_global_device_ids=true, to_apply=%region_11.0 | all-reduce | flops 32 | bytes 256 | tf_op jit(solution)/shard_map/psum | solution.py:82
  294.4 36.2 %all-reduce = (f32[3072]{0:T(1024)S(1)}, f32[3072]{0:T(1024)S(1)}) all-reduce(f32[3072]{0:T(1024)S(1)} %get-tuple-element.6, f32[3072]{0:T(1024)S(1)} %get-tuple-element.9), channel_id=1, replica_groups=mesh['row'=4,'col'=8] {'col'}, use_global_device_ids=true, to_apply=%region_16.0 | all-reduce | flops 6144 | bytes 49152 | tf_op jit(solution)/shard_map/psum | solution.py:88
  330.6 0.6 broadcast_multiply_fusion
  331.2 0.0 reduce-scatter.7.cloned.1.call-done
  331.2 0.0 copy-done.1
  331.2 1.7 fusion.23
  (3 shorter events, 0.0 us)
Async XLA Ops:
  7.2 47.8 %copy-start = (bf16[16,3072]{1,0:T(8,128)(2,1)S(1)}, bf16[16,3072]{1,0:T(8,128)(2,1)}, u32[]{:S(2)}) copy-start(bf16[16,3072]{1,0:T(8,128)(2,1)} %param.6) | copy-start | bytes 294916
  7.2 60.4 %copy-start.2 = (f32[3072]{0:T(1024)S(1)}, f32[3072]{0:T(1024)}, u32[]{:S(2)}) copy-start(f32[3072]{0:T(1024)} %param.7) | copy-start | bytes 36868
  7.2 60.4 %copy-start.3 = (f32[3072]{0:T(1024)S(1)}, f32[3072]{0:T(1024)}, u32[]{:S(2)}) copy-start(f32[3072]{0:T(1024)} %param.8) | copy-start | bytes 36868
  7.2 102.7 %reduce-scatter.9.cloned.1.call-start = ((), (), s32[]{:S(2)}) async-start(), calls=%async_computation.6 | async-start | bytes 983040 | tf_op jit(solution)/shard_map/reduce_scatter | solution.py:60
  54.9 78.5 %reduce-scatter.5.cloned.1.call-start = ((), (), s32[]{:S(2)}) async-start(), calls=%async_computation.4 | async-start | bytes 983040 | tf_op jit(solution)/shard_map/reduce_scatter | solution.py:42
  109.8 177.0 %reduce-scatter.11.cloned.1.call-start = ((), (), s32[]{:S(2)}) async-start(), calls=%async_computation.7 | async-start | bytes 884736 | tf_op jit(solution)/shard_map/reduce_scatter | solution.py:69
  180.7 150.5 %reduce-scatter.7.cloned.1.call-start = ((), (), s32[]{:S(2)}) async-start(), calls=%async_computation.5 | async-start | bytes 884736 | tf_op jit(solution)/shard_map/reduce_scatter | solution.py:50
  248.1 83.0 %copy-start.1 = (bf16[16,3072]{1,0:T(8,128)(2,1)S(1)}, bf16[16,3072]{1,0:T(8,128)(2,1)}, u32[]{:S(2)}) copy-start(bf16[16,3072]{1,0:T(8,128)(2,1)} %param.11) | copy-start | bytes 294916
Sparse Core Ops, SparseCore 0:
  55.0 24.1 reduce-scatter.8
  110.0 23.3 reduce-scatter.4
  180.8 62.8 reduce-scatter.10
  248.3 62.9 reduce-scatter.6
where the time goes:
time: 340 us; the launch traced here: 339 us
  blocking collectives  178 us (52%)
  matrix products  77.6 us (23%)
  other arithmetic  44 us (13%)
  waiting for transfers between devices  23.6 us (7%)
  between operations  15.9 us (5%)
    psum x1, blocking collectives, per_device(): lax.psum(jnp.sum(first * first) + jnp.sum(second * second), ('row', 'col'))  39.8 us
    convert_element_type x1, other arithmetic, per_device(): (second * factor).astype(jnp.bfloat16)  38.7 us
    psum x1, blocking collectives, per_device(): lax.psum((jnp.sum(grad_normed * normal, axis=0), jnp.sum(grad_normed, axi...  36.2 us
    all_gather x1, blocking collectives, per_device(): cotangent_all = lax.all_gather(cotangent, 'col', axis=0, tiled=True)  34 us
    all_gather x1, blocking collectives, per_device(): normed_all = lax.all_gather(normed, 'col', axis=0, tiled=True)  32.2 us
    dot_general x2, matrix products, transposed_product(): lax.dot_general(left, right, (((1,), (1,)), ((), ())), preferred_element_...  27.2 us
    reduce_scatter x1, waiting for transfers between devices, per_device(): lax.psum_scatter(jnp.dot(normed_all, weight_in, preferred_element_type=jn...  23.5 us
    dot_general x1, matrix products, per_device(): lax.dot_general(activation_all, cotangent_all, (((0,), (0,)), ((), ())),...  15.4 us
  transfers between devices with their start and end apart: 4, of which 1 were waited for; matrix products, arithmetic and copies ran while one was open for 22% of the time, Pallas kernels for 0%

commit v1 on v0

v1 whole, which is shorter than its diff:
```python
import functools

import jax
import jax.numpy as jnp
from jax import lax
from jax.experimental import pallas as pl
from jax.experimental.pallas import tpu as pltpu
from jax.sharding import PartitionSpec as P

gelu_scale = 0.7978845608028654
cubic = 0.044715
epsilon = 1e-05
CHUNK = 768
MESH = pl.DeviceIdType.MESH
f32, bf16 = jnp.float32, jnp.bfloat16


def chunk_of(width):
    return CHUNK if width % CHUNK == 0 else width


def remote(src, dst, send, recv, dev):
    return pltpu.make_async_remote_copy(
        src_ref=src, dst_ref=dst, send_sem=send, recv_sem=recv, device_id=dev, device_id_type=MESH
    )


class Axis:
    def __init__(self, name, size, total, device):
        self.size, self.half, self.outer = size, total // 2, size // 2
        self.piece = total // size
        self.me = lax.axis_index(name)
        self.o, self.i = self.me // 2, lax.rem(self.me, 2)
        self.device = device

    def out_peer(self, k):
        return lax.rem(self.o + k, self.outer)

    def out_source(self, k):
        return lax.rem(self.o + self.outer - k, self.outer)

    def dev(self, o, i):
        return self.device(o * 2 + i)

    def inner_dev(self):
        return self.dev(self.o, 1 - self.i)

    def rows(self, o, i):
        return pl.ds(pl.multiple_of(i * self.half + o * self.piece, self.piece), self.piece)

    def own(self):
        return self.rows(self.o, self.i)

    def half_rows(self, i):
        return pl.ds(pl.multiple_of(i * self.half, self.half), self.half)

    def in_half(self, o):
        return pl.ds(pl.multiple_of(o * self.piece, self.piece), self.piece)


class Gather:
    def __init__(self, axis, buf, sems):
        self.axis, self.buf = axis, buf
        self.osend, self.orecv, self.isend, self.irecv = sems

    def out_copy(self, n, k, source=False):
        a = self.axis
        o = a.out_source(k) if source else a.o
        ref = self.buf.at[n, a.rows(o, a.i)]
        return remote(ref, ref, self.osend.at[n, k], self.orecv.at[n, k], a.dev(a.out_peer(k), a.i))

    def in_copy(self, n, k, i):
        a = self.axis
        ref = self.buf.at[n, a.rows(a.out_source(k), i)]
        return remote(ref, ref, self.isend.at[n, k], self.irecv.at[n, k], a.inner_dev())

    def begin(self, n):
        for k in range(1, self.axis.outer):
            self.out_copy(n, k).start()
        self.in_copy(n, 0, self.axis.i).start()

    def forward(self, n):
        for k in range(1, self.axis.outer):
            self.out_copy(n, k, True).wait_recv()
            self.in_copy(n, k, self.axis.i).start()

    def finish(self, n):
        for k in range(self.axis.outer):
            self.in_copy(n, k, 1 - self.axis.i).wait_recv()

    def drain(self, n):
        for k in range(self.axis.outer):
            if k:
                self.out_copy(n, k).wait_send()
            self.in_copy(n, k, self.axis.i).wait_send()


class Scatter:
    def __init__(self, axis, part, half, out, sems):
        self.axis, self.part, self.half, self.out = axis, part, half, out
        self.isend, self.irecv, self.osend, self.orecv = sems

    def in_copy(self, n):
        a = self.axis
        return remote(
            self.part.at[n, a.half_rows(1 - a.i)], self.half.at[n],
            self.isend.at[n], self.irecv.at[n], a.inner_dev(),
        )

    def out_copy(self, n, k):
        a = self.axis
        return remote(
            self.half.at[n, a.in_half(a.out_peer(k))], self.out.at[n, k - 1],
            self.osend.at[n, k], self.orecv.at[n, k], a.dev(a.out_peer(k), a.i),
        )

    def begin(self, n, value):
        self.part[n] = value.astype(bf16)
        self.in_copy(n).start()

    def middle(self, n):
        a = self.axis
        self.in_copy(n).wait_recv()
        pair = self.part[n, a.half_rows(a.i), :].astype(f32) + self.half[n].astype(f32)
        self.half[n] = pair.astype(bf16)
        for k in range(1, a.outer):
            self.out_copy(n, k).start()

    def finish(self, n):
        a = self.axis
        total = self.half[n, a.in_half(a.o), :].astype(f32)
        for k in range(1, a.outer):
            self.out_copy(n, k).wait_recv()
            total = total + self.out[n, k - 1].astype(f32)
        return total

    def drain(self, n):
        self.in_copy(n).wait_send()
        for k in range(1, self.axis.outer):
            self.out_copy(n, k).wait_send()


class Direct:
    def __init__(self, axis, size, device, me, place, sems):
        self.size, self.device, self.me, self.place = size, device, me, place
        self.send, self.recv = sems

    def copy(self, k, source=False):
        slot = lax.rem(self.me + self.size - k, self.size) if source else self.me
        ref = self.place(slot)
        peer = self.device(lax.rem(self.me + k, self.size))
        return remote(ref, ref, self.send.at[k], self.recv.at[k], peer)

    def begin(self):
        for k in range(1, self.size):
            self.copy(k).start()

    def finish(self):
        for k in range(1, self.size):
            self.copy(k, True).wait_recv()

    def drain(self):
        for k in range(1, self.size):
            self.copy(k).wait_send()


def contract_last(left, right):
    return lax.dot_general(left, right, (((1,), (1,)), ((), ())), preferred_element_type=f32)


def two(first, second, shape):
    lane = lax.broadcasted_iota(jnp.int32, shape, 1)
    return jnp.where(lane < 64, jnp.broadcast_to(first, shape), jnp.broadcast_to(second, shape))


def exchange_kernel(
    n_row, n_col, nk, nh,
    tokens, gain, bias, win_hbm, wout_hbm, cot_own,
    normed_o, gh_o, act_o, cot_o, factor_o, output_o, igrad_o, gb_o,
    win, wout, tok, cot, normed, act, gh, slope, gn,
    part_h, part_g, part_m, part_n, half_h, half_g, half_m, half_n, out_h, out_g, out_m, out_n,
    rstat, stat, rsum, rsq, csq, gbx, gbz,
    wsem, osem,
    tok_a, tok_b, tok_c, tok_d, cot_a, cot_b, cot_c, cot_d,
    act_a, act_b, act_c, act_d, gh_a, gh_b, gh_c, gh_d,
    h_a, h_b, h_c, h_d, g_a, g_b, g_c, g_d, m_a, m_b, m_c, m_d, n_a, n_b, n_c, n_d,
    rs_a, rs_b, cs_a, cs_b, sum_a, sum_b, rq_a, rq_b, cq_a, cq_b, gx_a, gx_b, gz_a, gz_b,
):
    t0, width = tokens.shape
    total = t0 * n_col
    kc, hc = width // nk, win.shape[1] // nh
    features, hiddens = width * n_row, win.shape[1] * n_col
    my_row, my_col = lax.axis_index("row"), lax.axis_index("col")
    row_dev = lambda r: (r, my_col)
    col_dev = lambda c: (my_row, c)
    row = Axis("row", n_row, total, row_dev)
    col = Axis("col", n_col, total, col_dev)

    loads = []
    for index, (src, dst) in enumerate(((win_hbm, win), (wout_hbm, wout))):
        part = src.shape[0] // 4
        for q in range(4):
            rows = pl.ds(q * part, part)
            loads.append(pltpu.make_async_copy(src.at[rows], dst.at[rows], wsem.at[index * 4 + q]))
    for load in loads:
        load.start()

    barrier = pltpu.get_barrier_semaphore()
    for k in range(1, n_row):
        pl.semaphore_signal(barrier, inc=1, device_id=row_dev(lax.rem(my_row + k, n_row)), device_id_type=MESH)
    for k in range(1, n_col):
        pl.semaphore_signal(barrier, inc=1, device_id=col_dev(lax.rem(my_col + k, n_col)), device_id_type=MESH)

    for n in range(nk):
        tok[n, col.own(), :] = tokens[:, n * kc:(n + 1) * kc]
        cot[n, col.own(), :] = cot_own[:, n * kc:(n + 1) * kc]
    widened = tokens[...].astype(f32)
    local_mean = jnp.sum(widened, axis=1, keepdims=True) / width
    away = widened - local_mean
    rstat[my_row] = two(local_mean, jnp.sum(away * away, axis=1, keepdims=True), (t0, 128))
    pl.semaphore_wait(barrier, n_row + n_col - 2)

    tok_g = Gather(col, tok, (tok_a, tok_b, tok_c, tok_d))
    cot_g = Gather(col, cot, (cot_a, cot_b, cot_c, cot_d))
    act_g = Gather(row, act, (act_a, act_b, act_c, act_d))
    gh_g = Gather(row, gh, (gh_a, gh_b, gh_c, gh_d))
    h_s = Scatter(row, part_h, half_h, out_h, (h_a, h_b, h_c, h_d))
    g_s = Scatter(row, part_g, half_g, out_g, (g_a, g_b, g_c, g_d))
    m_s = Scatter(col, part_m, half_m, out_m, (m_a, m_b, m_c, m_d))
    n_s = Scatter(col, part_n, half_n, out_n, (n_a, n_b, n_c, n_d))
    rstat_d = Direct(row, n_row, row_dev, my_row, lambda s: rstat.at[s], (rs_a, rs_b))
    stat_d = Direct(col, n_col, col_dev, my_col, lambda s: stat.at[col.rows(s // 2, lax.rem(s, 2))], (cs_a, cs_b))
    sum_d = Direct(row, n_row, row_dev, my_row, lambda s: rsum.at[s], (sum_a, sum_b))
    rsq_d = Direct(row, n_row, row_dev, my_row, lambda s: rsq.at[s], (rq_a, rq_b))
    csq_d = Direct(col, n_col, col_dev, my_col, lambda s: csq.at[s], (cq_a, cq_b))
    gb_z = Direct(
        col, n_col // 2, lambda o: col.dev(o, col.i), col.o, lambda s: gbz.at[s], (gz_a, gz_b)
    )
    gb_x = remote(gbx.at[0], gbx.at[1], gx_a, gx_b, col.inner_dev())

    def each(count, body):
        def step(n, carry):
            body(n)
            return carry

        lax.fori_loop(0, count, step, 0)

    def keep(index, src, dst):
        copy = pltpu.make_async_copy(src, dst, osem.at[index])
        copy.start()
        return copy

    rstat_d.begin()
    each(nk, tok_g.begin)
    rstat_d.finish()
    means = [rstat[r][:, 0:1] for r in range(n_row)]
    mean = sum(means) / n_row
    spread = sum(rstat[r][:, 64:65] for r in range(n_row))
    spread = spread + width * sum((m - mean) * (m - mean) for m in means)
    own_inverse = lax.rsqrt(spread / features + epsilon)
    own_mean = mean
    stat[col.own(), :] = two(own_mean, own_inverse, (t0, 128))
    stat_d.begin()
    each(nk, tok_g.forward)
    each(nk, cot_g.begin)
    stat_d.finish()

    def normalize(n):
        tok_g.finish(n)
        normal = (tok[n].astype(f32) - stat[:, 0:1]) * stat[:, 64:65]
        normed[n] = (normal * gain[n] + bias[n]).astype(bf16)

    each(nk, normalize)
    kept = [keep(0, normed, normed_o)]
    for load in loads[:4]:
        load.wait()

    def forward_in(n):
        cols = pl.ds(pl.multiple_of(n * hc, hc), hc)
        h_s.begin(n, sum(
            jnp.dot(normed[k], win[k * kc:(k + 1) * kc, cols], preferred_element_type=f32) for k in range(nk)
        ))

    each(nh, forward_in)
    each(nh, h_s.middle)
    each(nk, cot_g.forward)

    def activate(n):
        v = h_s.finish(n)
        inner = jnp.tanh(gelu_scale * (v + cubic * v * v * v))
        slope[n] = 0.5 * (1.0 + inner) + 0.5 * v * (1.0 - inner * inner) * gelu_scale * (1.0 + 3.0 * cubic * v * v)
        act[n, row.own(), :] = (0.5 * v * (1.0 + inner)).astype(bf16)
        act_g.begin(n)

    each(nh, activate)
    each(nk, cot_g.finish)
    kept.append(keep(1, cot, cot_o))
    for load in loads[4:]:
        load.wait()

    def backward_out(n):
        rows = pl.ds(pl.multiple_of(n * hc, hc), hc)
        g_s.begin(n, sum(contract_last(cot[k], wout[rows, k * kc:(k + 1) * kc]) for k in range(nk)))

    each(nh, backward_out)
    each(nh, act_g.forward)
    each(nh, g_s.middle)
    each(nh, act_g.finish)
    kept.append(keep(2, act, act_o))

    def forward_out(n):
        cols = pl.ds(pl.multiple_of(n * kc, kc), kc)
        m_s.begin(n, sum(
            jnp.dot(act[k], wout[k * hc:(k + 1) * hc, cols], preferred_element_type=f32) for k in range(nh)
        ))

    each(nk, forward_out)

    def slope_times(n):
        gh[n, row.own(), :] = (g_s.finish(n) * slope[n]).astype(bf16)
        gh_g.begin(n)

    each(nh, slope_times)
    each(nk, m_s.middle)
    gram_normed = sum(contract_last(normed[k], normed[k]) for k in range(nk))
    gram_cot = sum(contract_last(cot[k], cot[k]) for k in range(nk))
    gram_act = sum(contract_last(act[k], act[k]) for k in range(nh))
    each(nh, gh_g.forward)
    each(nh, gh_g.finish)
    kept.append(keep(3, gh, gh_o))
    gram_gh = sum(contract_last(gh[k], gh[k]) for k in range(nh))
    products = gram_normed * gram_gh + gram_act * gram_cot
    rsq[my_row] = jnp.broadcast_to(jnp.sum(jnp.sum(products, axis=1, keepdims=True), axis=0, keepdims=True), (8, 128))
    rsq_d.begin()

    if gbx.shape[1] > 2 * nk:
        gbx[0] = jnp.zeros_like(gbx[0])

    def backward_in(n):
        rows = pl.ds(pl.multiple_of(n * kc, kc), kc)
        value = sum(contract_last(gh[k], win[rows, k * hc:(k + 1) * hc]) for k in range(nh))
        n_s.begin(n, value)
        normal = (tok[n].astype(f32) - stat[:, 0:1]) * stat[:, 64:65]
        gbx[0, pl.ds(n, 1), :] = jnp.sum(value * normal, axis=0, keepdims=True)
        gbx[0, pl.ds(nk + n, 1), :] = jnp.sum(value, axis=0, keepdims=True)

    each(nk, backward_in)
    rsq_d.finish()
    csq[my_col] = sum(rsq[r] for r in range(n_row))
    csq_d.begin()
    gb_x.start()
    each(nk, n_s.middle)
    gb_x.wait_recv()
    gbz[col.o] = gbx[0] + gbx[1]
    gb_z.begin()

    for n in range(nk):
        mixed = m_s.finish(n)
        output_o[:, n * kc:(n + 1) * kc] = (tokens[:, n * kc:(n + 1) * kc].astype(f32) + mixed).astype(bf16)

    one = jnp.zeros((t0, 1), f32)
    other = jnp.zeros((t0, 1), f32)
    for n in range(nk):
        grad_normed = n_s.finish(n)
        normal = (tokens[:, n * kc:(n + 1) * kc].astype(f32) - own_mean) * own_inverse
        scaled = grad_normed * gain[n]
        gn[n] = scaled
        one = one + jnp.sum(scaled, axis=1, keepdims=True)
        other = other + jnp.sum(scaled * normal, axis=1, keepdims=True)
    rsum[my_row] = two(one, other, (t0, 128))
    sum_d.begin()

    csq_d.finish()
    squares = jnp.maximum(sum(csq[c] for c in range(n_col)), 0.0)
    factor = jnp.minimum(1.0, jnp.sqrt(2.0 * features * hiddens / squares))
    factor_o[...] = factor
    gb_z.finish()
    gb_o[...] = sum(gbz[o] for o in range(n_col // 2)) * factor[0:1, 0:1]
    sum_d.finish()
    sums = sum(rsum[r] for r in range(n_row))
    for n in range(nk):
        cols = slice(n * kc, (n + 1) * kc)
        normal = (tokens[:, cols].astype(f32) - own_mean) * own_inverse
        igrad_o[:, cols] = (
            cot_own[:, cols].astype(f32)
            + own_inverse * (gn[n] - sums[:, 0:1] / features - normal * (sums[:, 64:65] / features))
        ).astype(bf16)

    for gather, count in ((tok_g, nk), (cot_g, nk), (act_g, nh), (gh_g, nh)):
        each(count, gather.drain)
    for scatter, count in ((h_s, nh), (g_s, nh), (m_s, nk), (n_s, nk)):
        each(count, scatter.drain)
    for direct in (rstat_d, stat_d, sum_d, rsq_d, csq_d, gb_z):
        direct.drain()
    gb_x.wait_send()
    for copy in kept:
        copy.wait()


def gradient_kernel(
    nk, nh, normed, gh, act, cot, factor, output, igrad, gb,
    first_o, second_o, output_o, igrad_o, gain_o, bias_o,
):
    @pl.when(pl.program_id(0) == 0)
    def _():
        output_o[...] = output[...]
        igrad_o[...] = igrad[...]
        gain_o[...] = gb[0:nk, :]
        bias_o[...] = gb[nk:2 * nk, :]

    scale = factor[0:1, 0:1]
    for left, right, out in ((normed, gh, first_o), (act, cot, second_o)):
        flipped = left[0].T
        piece = right.shape[2]
        for j in range(right.shape[0]):
            value = jnp.dot(flipped, right[j], preferred_element_type=f32)
            out[:, j * piece:(j + 1) * piece] = (value * scale).astype(bf16)


def per_device(n_row, n_col, tokens, norm_gain, norm_bias, weight_in, weight_out, cotangent):
    t0, width = tokens.shape
    hidden = weight_in.shape[1]
    total = t0 * n_col
    kc, hc = chunk_of(width), chunk_of(hidden)
    nk, nh = width // kc, hidden // hc
    ro, co = n_row // 2, n_col // 2
    rp, cp = total // n_row, total // n_col
    gb_rows = max(8, 2 * nk)
    gain = norm_gain.reshape(nk, 1, kc)
    bias = norm_bias.reshape(nk, 1, kc)
    vmem = pl.BlockSpec(memory_space=pltpu.VMEM)
    anywhere = pl.BlockSpec(memory_space=pl.ANY)
    V = pltpu.VMEM
    dma = pltpu.SemaphoreType.DMA
    wide, deep = (nk, total, kc), (nh, total, hc)

    def gather_sems(count, outer):
        return [dma((count, outer))] * 4

    def scatter_sems(count, outer):
        return [dma((count,)), dma((count,)), dma((count, outer)), dma((count, outer))]

    scratch = [
        V((width, hidden), bf16), V((hidden, width), bf16),
        V(wide, bf16), V(wide, bf16), V(wide, bf16), V(deep, bf16), V(deep, bf16),
        V((nh, rp, hc), f32), V((nk, cp, kc), f32),
        V(deep, bf16), V(deep, bf16), V(wide, bf16), V(wide, bf16),
        V((nh, total // 2, hc), bf16), V((nh, total // 2, hc), bf16),
        V((nk, total // 2, kc), bf16), V((nk, total // 2, kc), bf16),
        V((nh, max(1, ro - 1), rp, hc), bf16), V((nh, max(1, ro - 1), rp, hc), bf16),
        V((nk, max(1, co - 1), cp, kc), bf16), V((nk, max(1, co - 1), cp, kc), bf16),
        V((n_row, t0, 128), f32), V((total, 128), f32), V((n_row, t0, 128), f32),
        V((n_row, 8, 128), f32), V((n_col, 8, 128), f32),
        V((2, gb_rows, kc), f32), V((co, gb_rows, kc), f32),
        dma((8,)), dma((4,)),
        *gather_sems(nk, co), *gather_sems(nk, co), *gather_sems(nh, ro), *gather_sems(nh, ro),
        *scatter_sems(nh, ro), *scatter_sems(nh, ro), *scatter_sems(nk, co), *scatter_sems(nk, co),
        dma((n_row,)), dma((n_row,)), dma((n_col,)), dma((n_col,)), dma((n_row,)), dma((n_row,)),
        dma((n_row,)), dma((n_row,)), dma((n_col,)), dma((n_col,)), dma, dma, dma((co,)), dma((co,)),
    ]
    S = jax.ShapeDtypeStruct
    mid = pl.pallas_call(
        functools.partial(exchange_kernel, n_row, n_col, nk, nh),
        out_shape=[
            S(wide, bf16), S(deep, bf16), S(deep, bf16), S(wide, bf16), S((8, 128), f32),
            S((t0, width), bf16), S((t0, width), bf16), S((gb_rows, kc), f32),
        ],
        in_specs=[vmem, vmem, vmem, anywhere, anywhere, vmem],
        out_specs=[anywhere] * 4 + [vmem] * 4,
        scratch_shapes=scratch,
        compiler_params=pltpu.CompilerParams(
            collective_id=0, has_side_effects=True, vmem_limit_bytes=60 * 2**20
        ),
    )(tokens, gain, bias, weight_in, weight_out, cotangent)
    tile = 256
    steps = width // tile
    per_k, per_h = kc // tile, hc // tile
    whole = lambda shape: pl.BlockSpec(shape, lambda i: (0,) * len(shape))
    first, second, output, igrad, gain_grad, bias_grad = pl.pallas_call(
        functools.partial(gradient_kernel, nk, nh),
        grid=(steps,),
        out_shape=[
            S((width, hidden), bf16), S((hidden, width), bf16), S((t0, width), bf16), S((t0, width), bf16),
            S((nk, kc), f32), S((nk, kc), f32),
        ],
        in_specs=[
            pl.BlockSpec((1, total, tile), lambda i: (i // per_k, 0, i % per_k)), whole(deep),
            pl.BlockSpec((1, total, tile), lambda i: (i // per_h, 0, i % per_h)), whole(wide),
            whole((8, 128)), whole((t0, width)), whole((t0, width)), whole((gb_rows, kc)),
        ],
        out_specs=[
            pl.BlockSpec((tile, hidden), lambda i: (i, 0)), pl.BlockSpec((hidden // steps, width), lambda i: (i, 0)),
            whole((t0, width)), whole((t0, width)), whole((nk, kc)), whole((nk, kc)),
        ],
        compiler_params=pltpu.CompilerParams(vmem_limit_bytes=40 * 2**20),
    )(*mid)
    return output, igrad, first, second, gain_grad.reshape(width), bias_grad.reshape(width)


def solution(mesh):
    specs = (P("col", "row"), P("row"), P("row"), P("row", "col"), P("col", "row"), P("col", "row"))
    return jax.shard_map(
        functools.partial(per_device, mesh.shape["row"], mesh.shape["col"]),
        mesh=mesh,
        in_specs=specs,
        out_specs=(P("col", "row"), P("col", "row"), P("row", "col"), P("col", "row"), P("row"), P("row")),
        check_vma=False,
    )
```

time: 340 us -> 106 us (0.31)
  blocking collectives: 178 us -> 0 us
  Pallas kernels: 0 us -> 95.8 us
  matrix products: 77.6 us -> 0 us
  other arithmetic: 44 us -> 0 us
  waiting for transfers between devices: 23.6 us -> 0 us
  between operations: 15.9 us -> 0.66 us
  local copies, waits for them, and re-layouts: 0.02 us -> 8.95 us
    pallas_call x0 -> x2, Pallas kernels: none -> 95.8 us  [the longest x1 81.3 us: per_device(): pl.pallas_call(functools.partial(exchange_kernel, n_row, n_col, nk, nh),...]
    psum x5 -> x0, blocking collectives: 94.6 us -> none  [the longest x1 39.8 us: per_device(): lax.psum(jnp.sum(first * first) + jnp.sum(second * second), ('row', 'col'))]
    all_gather x4 -> x0, blocking collectives: 83.4 us -> none  [the longest x1 34 us: per_device(): cotangent_all = lax.all_gather(cotangent, 'col', axis=0, tiled=True)]
    dot_general x6 -> x0, matrix products: 77.6 us -> none  [the longest x2 27.2 us: transposed_product(): lax.dot_general(left, right, (((1,), (1,)), ((), ())), preferred_element_...]
    convert_element_type x4 -> x0, other arithmetic: 41.8 us -> none  [the longest x1 38.7 us: per_device(): (second * factor).astype(jnp.bfloat16)]
    reduce_scatter x4 -> x0, waiting for transfers between devices: 23.5 us -> none  [the longest x1 23.5 us: per_device(): lax.psum_scatter(jnp.dot(normed_all, weight_in, preferred_element_type=jn...]
    unnamed x8 -> x16, local copies, waits for them, and re-layouts: 0.02 us -> 7.73 us
  transfers between devices with their start and end apart: 4 -> 0, of which waited for: 1 -> 0; matrix products, arithmetic and copies ran while one was open for 22% -> 0% of each run, Pallas kernels for 0% -> 0%
where the time goes in v1:
time: 106 us; the launch traced here: 105 us
  Pallas kernels  95.8 us (90%)
  local copies, waits for them, and re-layouts  8.95 us (8%)
    pallas_call x1, Pallas kernels, per_device(): pl.pallas_call(functools.partial(exchange_kernel, n_row, n_col, nk, nh),...  81.3 us
    pallas_call x1, Pallas kernels, per_device(): pl.pallas_call(functools.partial(gradient_kernel, nk, nh), grid=(steps,),...  14.5 us
    unnamed x16, local copies, waits for them, and re-layouts  7.73 us

profile of v1, /device:TPU:0, one launch (start us, length us, event | category | flops | bytes accessed | tf_op | source)
XLA Modules:
  0.0 105.4 jit_solution(1704182504240976987)
XLA Ops:
  0.6 81.3 %shard_map.109 = (bf16[4,128,768]{2,1,0:T(8,128)(2,1)}, bf16[4,128,768]{2,1,0:T(8,128)(2,1)}, bf16[4,128,768]{2,1,0:T(8,128)(2,1)}, bf16[4,128,768]{2,1,0:T(8,12...) custom-call(bf16[16,3072]{1,0:T(8,128)(2,1)} %tokens.1, ...), custom_call_target="tpu_custom_call" | custom-call | tf_op jit(solution)/shard_map/pallas_call | solution.py:462
  82.0 0.0 copy-start
  82.0 1.1 %copy-done = bf16[4,128,768]{2,1,0:T(8,128)(2,1)S(1)} copy-done((bf16[4,128,768]{2,1,0:T(8,128)(2,1)S(1)}, bf16[4,128,768]{2,1,0:T(8,128)(2,1)}, u32[]{:S(2)}) %copy-start) | copy-done | bytes 786456
  83.1 0.0 copy-start.1
  83.1 1.1 %copy-done.1 = bf16[4,128,768]{2,1,0:T(8,128)(2,1)S(1)} copy-done((bf16[4,128,768]{2,1,0:T(8,128)(2,1)S(1)}, bf16[4,128,768]{2,1,0:T(8,128)(2,1)}, u32[]{:S(2)}) %copy-start.1) | copy-done | bytes 786456
  84.2 0.0 copy-start.2
  84.2 1.1 %copy-done.2 = bf16[4,128,768]{2,1,0:T(8,128)(2,1)S(1)} copy-done((bf16[4,128,768]{2,1,0:T(8,128)(2,1)S(1)}, bf16[4,128,768]{2,1,0:T(8,128)(2,1)}, u32[]{:S(2)}) %copy-start.2) | copy-done | bytes 786456
  85.4 0.0 copy-start.3
  85.4 1.1 %copy-done.3 = bf16[4,128,768]{2,1,0:T(8,128)(2,1)S(1)} copy-done((bf16[4,128,768]{2,1,0:T(8,128)(2,1)S(1)}, bf16[4,128,768]{2,1,0:T(8,128)(2,1)}, u32[]{:S(2)}) %copy-start.3) | copy-done | bytes 786456
  86.5 0.0 copy-start.4
  86.5 0.9 copy-done.4
  87.4 0.0 copy-start.5
  87.4 0.9 copy-done.5
  88.3 0.0 copy-start.6
  88.3 0.7 copy-done.6
  89.0 0.0 copy-start.7
  89.0 0.7 copy-done.7
  89.7 14.5 %shard_map.110 = (bf16[3072,3072]{1,0:T(8,128)(2,1)}, bf16[3072,3072]{1,0:T(8,128)(2,1)}, bf16[16,3072]{1,0:T(8,128)(2,1)}, bf16[16,3072]{1,0:T(8,128)(2,1)}, f3...) custom-call(bf16[4,128,768]{2,1,0:T(8,128)(2,1)S(1)} %copy-done, bf16[4,128,768]{2,1,0:T(8,128)(2,1)S(1)} %copy-done.1, ...), custom_call_target="tpu_custom_call" | custom-call | tf_op jit(solution)/shard_map/pallas_call | solution.py:479
  104.2 0.6 reshape.26
  104.8 0.6 reshape.27
Async XLA Ops:
  82.0 1.1 %copy-start = (bf16[4,128,768]{2,1,0:T(8,128)(2,1)S(1)}, bf16[4,128,768]{2,1,0:T(8,128)(2,1)}, u32[]{:S(2)}) copy-start(bf16[4,128,768]{2,1,0:T(8,128)(2,1)} %get-tuple-element.20.normed) | copy-start | bytes 2359300
  83.1 1.1 %copy-start.1 = (bf16[4,128,768]{2,1,0:T(8,128)(2,1)S(1)}, bf16[4,128,768]{2,1,0:T(8,128)(2,1)}, u32[]{:S(2)}) copy-start(bf16[4,128,768]{2,1,0:T(8,128)(2,1)} %get-tuple-element.21.gh) | copy-start | bytes 2359300
  84.2 1.1 %copy-start.2 = (bf16[4,128,768]{2,1,0:T(8,128)(2,1)S(1)}, bf16[4,128,768]{2,1,0:T(8,128)(2,1)}, u32[]{:S(2)}) copy-start(bf16[4,128,768]{2,1,0:T(8,128)(2,1)} %get-tuple-element.22.act) | copy-start | bytes 2359300
  85.4 1.1 %copy-start.3 = (bf16[4,128,768]{2,1,0:T(8,128)(2,1)S(1)}, bf16[4,128,768]{2,1,0:T(8,128)(2,1)}, u32[]{:S(2)}) copy-start(bf16[4,128,768]{2,1,0:T(8,128)(2,1)} %get-tuple-element.23.cot) | copy-start | bytes 2359300
  86.5 0.9 copy-start.4
  87.4 0.9 copy-start.5
  88.3 0.7 copy-start.6
  89.0 0.7 copy-start.7

commit v2 on v1

--- a/solution.py
+++ b/solution.py
@@ -179,7 +179,7 @@
     normed_o, gh_o, act_o, cot_o, factor_o, output_o, igrad_o, gb_o,
     win, wout, tok, cot, normed, act, gh, slope, gn,
     part_h, part_g, part_m, part_n, half_h, half_g, half_m, half_n, out_h, out_g, out_m, out_n,
-    rstat, stat, rsum, rsq, csq, gbx, gbz,
+    acc, rstat, stat, rsum, rsq, csq, gbx, gbz,
     wsem, osem,
     tok_a, tok_b, tok_c, tok_d, cot_a, cot_b, cot_c, cot_d,
     act_a, act_b, act_c, act_d, gh_a, gh_b, gh_c, gh_d,
@@ -198,10 +198,11 @@
 
     loads = []
     for index, (src, dst) in enumerate(((win_hbm, win), (wout_hbm, wout))):
-        part = src.shape[0] // 4
-        for q in range(4):
+        pieces = 4 if index else nk
+        part = src.shape[0] // pieces
+        for q in range(pieces):
             rows = pl.ds(q * part, part)
-            loads.append(pltpu.make_async_copy(src.at[rows], dst.at[rows], wsem.at[index * 4 + q]))
+            loads.append(pltpu.make_async_copy(src.at[rows], dst.at[rows], wsem.at[index * nk + q]))
     for load in loads:
         load.start()
 
@@ -245,6 +246,40 @@
 
         lax.fori_loop(0, count, step, 0)
 
+    def stream(count, ready, term, columns, scatter, extra=None):
+        if count > 1:
+            for n in range(columns):
+                acc[n] = jnp.zeros_like(acc[n])
+
+        def step(k):
+            ready(k)
+            for n in range(columns):
+                acc[n] += term(k, n)
+
+        each(count - 1, step)
+        ready(count - 1)
+        for n in range(columns):
+            value = term(count - 1, n)
+            if count > 1:
+                value = value + acc[n]
+            scatter.begin(n, value)
+            if extra is not None:
+                extra(n, value)
+
+    def chunk(k, size):
+        return pl.ds(k * size if isinstance(k, int) else pl.multiple_of(k * size, size), size)
+
+    def ahead(gather, count):
+        def ready(k):
+            if isinstance(k, int):
+                gather.finish(k)
+            else:
+                gather.forward(k + 1)
+                gather.finish(k)
+
+        gather.forward(0)
+        return ready
+
     def keep(index, src, dst):
         copy = pltpu.make_async_copy(src, dst, osem.at[index])
         copy.start()
@@ -267,21 +302,16 @@
 
     def normalize(n):
         tok_g.finish(n)
+        pltpu.make_async_copy(win_hbm.at[chunk(n, kc)], win.at[chunk(n, kc)], wsem.at[n]).wait()
         normal = (tok[n].astype(f32) - stat[:, 0:1]) * stat[:, 64:65]
         normed[n] = (normal * gain[n] + bias[n]).astype(bf16)
 
-    each(nk, normalize)
+    stream(
+        nk, normalize,
+        lambda k, n: jnp.dot(normed[k], win[chunk(k, kc), n * hc:(n + 1) * hc], preferred_element_type=f32),
+        nh, h_s,
+    )
     kept = [keep(0, normed, normed_o)]
-    for load in loads[:4]:
-        load.wait()
-
-    def forward_in(n):
-        cols = pl.ds(pl.multiple_of(n * hc, hc), hc)
-        h_s.begin(n, sum(
-            jnp.dot(normed[k], win[k * kc:(k + 1) * kc, cols], preferred_element_type=f32) for k in range(nk)
-        ))
-
-    each(nh, forward_in)
     each(nh, h_s.middle)
     each(nk, cot_g.forward)
 
@@ -293,66 +323,62 @@
         act_g.begin(n)
 
     each(nh, activate)
-    each(nk, cot_g.finish)
+    for load in loads[nk:]:
+        load.wait()
+    stream(
+        nk, cot_g.finish,
+        lambda k, n: contract_last(cot[k], wout[n * hc:(n + 1) * hc, chunk(k, kc)]),
+        nh, g_s,
+    )
     kept.append(keep(1, cot, cot_o))
-    for load in loads[4:]:
-        load.wait()
-
-    def backward_out(n):
-        rows = pl.ds(pl.multiple_of(n * hc, hc), hc)
-        g_s.begin(n, sum(contract_last(cot[k], wout[rows, k * kc:(k + 1) * kc]) for k in range(nk)))
-
-    each(nh, backward_out)
     each(nh, act_g.forward)
     each(nh, g_s.middle)
-    each(nh, act_g.finish)
+    stream(
+        nh, act_g.finish,
+        lambda k, n: jnp.dot(act[k], wout[chunk(k, hc), n * kc:(n + 1) * kc], preferred_element_type=f32),
+        nk, m_s,
+    )
     kept.append(keep(2, act, act_o))
-
-    def forward_out(n):
-        cols = pl.ds(pl.multiple_of(n * kc, kc), kc)
-        m_s.begin(n, sum(
-            jnp.dot(act[k], wout[k * hc:(k + 1) * hc, cols], preferred_element_type=f32) for k in range(nh)
-        ))
-
-    each(nk, forward_out)
 
     def slope_times(n):
         gh[n, row.own(), :] = (g_s.finish(n) * slope[n]).astype(bf16)
         gh_g.begin(n)
 
     each(nh, slope_times)
-    each(nk, m_s.middle)
     gram_normed = sum(contract_last(normed[k], normed[k]) for k in range(nk))
     gram_cot = sum(contract_last(cot[k], cot[k]) for k in range(nk))
     gram_act = sum(contract_last(act[k], act[k]) for k in range(nh))
-    each(nh, gh_g.forward)
-    each(nh, gh_g.finish)
+    if gbx.shape[1] > 2 * nk:
+        gbx[0] = jnp.zeros_like(gbx[0])
+
+    def over_tokens(n, value):
+        normal = (tok[n].astype(f32) - stat[:, 0:1]) * stat[:, 64:65]
+        gbx[0, n:n + 1, :] = jnp.sum(value * normal, axis=0, keepdims=True)
+        gbx[0, nk + n:nk + n + 1, :] = jnp.sum(value, axis=0, keepdims=True)
+
+    stream(
+        nh, ahead(gh_g, nh),
+        lambda k, n: contract_last(gh[k], win[n * kc:(n + 1) * kc, chunk(k, hc)]),
+        nk, n_s, over_tokens,
+    )
     kept.append(keep(3, gh, gh_o))
+    gb_x.start()
     gram_gh = sum(contract_last(gh[k], gh[k]) for k in range(nh))
     products = gram_normed * gram_gh + gram_act * gram_cot
     rsq[my_row] = jnp.broadcast_to(jnp.sum(jnp.sum(products, axis=1, keepdims=True), axis=0, keepdims=True), (8, 128))
     rsq_d.begin()
-
-    if gbx.shape[1] > 2 * nk:
-        gbx[0] = jnp.zeros_like(gbx[0])
-
-    def backward_in(n):
-        rows = pl.ds(pl.multiple_of(n * kc, kc), kc)
-        value = sum(contract_last(gh[k], win[rows, k * hc:(k + 1) * hc]) for k in range(nh))
-        n_s.begin(n, value)
-        normal = (tok[n].astype(f32) - stat[:, 0:1]) * stat[:, 64:65]
-        gbx[0, pl.ds(n, 1), :] = jnp.sum(value * normal, axis=0, keepdims=True)
-        gbx[0, pl.ds(nk + n, 1), :] = jnp.sum(value, axis=0, keepdims=True)
-
-    each(nk, backward_in)
+    each(nk, m_s.middle)
+    each(nk, n_s.middle)
     rsq_d.finish()
     csq[my_col] = sum(rsq[r] for r in range(n_row))
     csq_d.begin()
-    gb_x.start()
-    each(nk, n_s.middle)
     gb_x.wait_recv()
     gbz[col.o] = gbx[0] + gbx[1]
     gb_z.begin()
+    for gather, count in ((tok_g, nk), (cot_g, nk), (act_g, nh), (gh_g, nh)):
+        each(count, gather.drain)
+    for scatter, count in ((h_s, nh), (g_s, nh)):
+        each(count, scatter.drain)
 
     for n in range(nk):
         mixed = m_s.finish(n)
@@ -386,10 +412,8 @@
             + own_inverse * (gn[n] - sums[:, 0:1] / features - normal * (sums[:, 64:65] / features))
         ).astype(bf16)
 
-    for gather, count in ((tok_g, nk), (cot_g, nk), (act_g, nh), (gh_g, nh)):
-        each(count, gather.drain)
-    for scatter, count in ((h_s, nh), (g_s, nh), (m_s, nk), (n_s, nk)):
-        each(count, scatter.drain)
+    for scatter in (m_s, n_s):
+        each(nk, scatter.drain)
     for direct in (rstat_d, stat_d, sum_d, rsq_d, csq_d, gb_z):
         direct.drain()
     gb_x.wait_send()
@@ -405,8 +429,10 @@
     def _():
         output_o[...] = output[...]
         igrad_o[...] = igrad[...]
-        gain_o[...] = gb[0:nk, :]
-        bias_o[...] = gb[nk:2 * nk, :]
+        kc = gb.shape[1]
+        for n in range(nk):
+            gain_o[n * kc:(n + 1) * kc] = gb[n, :]
+            bias_o[n * kc:(n + 1) * kc] = gb[nk + n, :]
 
     scale = factor[0:1, 0:1]
     for left, right, out in ((normed, gh, first_o), (act, cot, second_o)):
@@ -449,10 +475,11 @@
         V((nk, total // 2, kc), bf16), V((nk, total // 2, kc), bf16),
         V((nh, max(1, ro - 1), rp, hc), bf16), V((nh, max(1, ro - 1), rp, hc), bf16),
         V((nk, max(1, co - 1), cp, kc), bf16), V((nk, max(1, co - 1), cp, kc), bf16),
+        V((max(nk, nh), total, max(kc, hc)), f32),
         V((n_row, t0, 128), f32), V((total, 128), f32), V((n_row, t0, 128), f32),
         V((n_row, 8, 128), f32), V((n_col, 8, 128), f32),
         V((2, gb_rows, kc), f32), V((co, gb_rows, kc), f32),
-        dma((8,)), dma((4,)),
+        dma((nk + 4,)), dma((4,)),
         *gather_sems(nk, co), *gather_sems(nk, co), *gather_sems(nh, ro), *gather_sems(nh, ro),
         *scatter_sems(nh, ro), *scatter_sems(nh, ro), *scatter_sems(nk, co), *scatter_sems(nk, co),
         dma((n_row,)), dma((n_row,)), dma((n_col,)), dma((n_col,)), dma((n_row,)), dma((n_row,)),
@@ -481,7 +508,7 @@
         grid=(steps,),
         out_shape=[
             S((width, hidden), bf16), S((hidden, width), bf16), S((t0, width), bf16), S((t0, width), bf16),
-            S((nk, kc), f32), S((nk, kc), f32),
+            S((width,), f32), S((width,), f32),
         ],
         in_specs=[
             pl.BlockSpec((1, total, tile), lambda i: (i // per_k, 0, i % per_k)), whole(deep),
@@ -490,11 +517,11 @@
         ],
         out_specs=[
             pl.BlockSpec((tile, hidden), lambda i: (i, 0)), pl.BlockSpec((hidden // steps, width), lambda i: (i, 0)),
-            whole((t0, width)), whole((t0, width)), whole((nk, kc)), whole((nk, kc)),
+            whole((t0, width)), whole((t0, width)), whole((width,)), whole((width,)),
         ],
-        compiler_params=pltpu.CompilerParams(vmem_limit_bytes=40 * 2**20),
+        compiler_params=pltpu.CompilerParams(vmem_limit_bytes=60 * 2**20),
     )(*mid)
-    return output, igrad, first, second, gain_grad.reshape(width), bias_grad.reshape(width)
+    return output, igrad, first, second, gain_grad, bias_grad
 
 
 def solution(mesh):

time: 106 us -> 99.3 us (0.937)
  local copies, waits for them, and re-layouts: 8.95 us -> 0 us
  Pallas kernels: 95.8 us -> 98.3 us
    unnamed x16 -> x0, local copies, waits for them, and re-layouts: 7.73 us -> none
    pallas_call x1, Pallas kernels: 14.5 us -> 16 us  [per_device(): pl.pallas_call(functools.partial(gradient_kernel, nk, nh), grid=(steps,),...]
    reshape x2 -> x0, local copies, waits for them, and re-layouts: 1.22 us -> none  [the longest x1 0.61 us: per_device(): gain_grad.reshape(width)]
where the time goes in v2:
time: 99.3 us; the launch traced here: 98.9 us
  Pallas kernels  98.3 us (99%)
    pallas_call x1, Pallas kernels, per_device(): pl.pallas_call(functools.partial(exchange_kernel, n_row, n_col, nk, nh),...  82.3 us
    pallas_call x1, Pallas kernels, per_device(): pl.pallas_call(functools.partial(gradient_kernel, nk, nh), grid=(steps,),...  16 us

profile of v2, /device:TPU:0, one launch (start us, length us, event | category | flops | bytes accessed | tf_op | source)
XLA Modules:
  0.0 98.9 jit_solution(8487145224123934380)
XLA Ops:
  0.6 82.3 %shard_map.109 = (bf16[4,128,768]{2,1,0:T(8,128)(2,1)}, bf16[4,128,768]{2,1,0:T(8,128)(2,1)}, bf16[4,128,768]{2,1,0:T(8,128)(2,1)}, bf16[4,128,768]{2,1,0:T(8,12...) custom-call(bf16[16,3072]{1,0:T(8,128)(2,1)} %tokens.1, ...), custom_call_target="tpu_custom_call" | custom-call | tf_op jit(solution)/shard_map/pallas_call | solution.py:489
  82.9 16.0 %shard_map.110 = (bf16[3072,3072]{1,0:T(8,128)(2,1)}, bf16[3072,3072]{1,0:T(8,128)(2,1)}, bf16[16,3072]{1,0:T(8,128)(2,1)}, bf16[16,3072]{1,0:T(8,128)(2,1)}, f32[3072]{0:T(1024)}, /*index=5*/f32[3072]{0:T(1024)}) custom-call(bf16[4,128,768]{2,1,0:T(8,128)(2,1)} %get-tuple-element.20.normed, bf16[4,128,768]{2,1,0:T(8,128)(2,1)} %get-tuple-element.21.gh, ...), custom_call_target="tpu_custom_call" | custom-call | tf_op jit(solution)/shard_map/pallas_call | solution.py:506
